TPU v7x, 32 devices: a whole 2x2x4 slice. The times are simulated.
32 devices in a mesh: gx: 2 (over core), gz: 16 (over z, y, x).
Axes of the slice: x: 2, y: 2, z: 4, core: 2. Of those that a mesh axis runs over, the one named last changes fastest.
Arguments:
- modes: bfloat16 [3, 4, 128, 128, 128], P(None, 'gx', None, 'gz'), may hold values from -6 to 6
- weights: float32 [4, 128, 128], P('gx', None, 'gz'), may hold values from 0.0022552917 to 0.022552917
- counts: int32 [32], P(('gx', 'gz')), may hold values from 1 to 128, 1365 in all
- mode_index: int32 [16], replicated, may hold values from 0 to 127, as said below
Outputs:
- slices: float32 [16, 128, 128], P(None, 'gz')
Inputs may be any that keep to these rules, and one draw needn't show every extreme that they name: `mode_index`: distinct modes. The counts sum to 128 * 2 * 16 // 3 and one pencil holds 128.
All inputs are finite; a program needn't handle non-finite values. No bound on the sum of `counts` on one device may be relied on, other than what follows from the above.
Results may differ from a plain program's by a relative error of at most 0.004.
Values may be sent and summed in bfloat16 or wider, within the bound.
No kernel may reach another device: no remote copies, remote signals or barrier semaphores. Data moves between devices by JAX's collectives and lax.ppermute only.
A program may use at most 64 MiB of HBM per device.

v0:
```python
import jax
import jax.numpy as jnp
from jax import lax
from jax.sharding import PartitionSpec as P

YBLK = 8


def padded_2(block, sides, width):
    for axis, dim in sides:
        count = lax.axis_size(axis)
        forward = [(i, i + 1) for i in range(count - 1)]
        forward.append((count - 1, 0))
        backward = [(target, source) for source, target in forward]
        low = lax.ppermute(
            lax.slice_in_dim(block, block.shape[dim] - width, None, axis=dim), axis, forward
        )
        high = lax.ppermute(lax.slice_in_dim(block, 0, width, axis=dim), axis, backward)
        block = jnp.concatenate([low, block, high], axis=dim)
    return block


def region_terms(source, weight_part, live_count, onehot, running):
    size_m = source.shape[4]
    span_x = source.shape[1] - 2
    level_cap = source.shape[2]
    span_z = source.shape[3] - 2
    points = span_x * YBLK * span_z
    highest = lax.Precision.HIGHEST
    padded = jnp.pad(source, ((0, 0), (0, 0), (1, 1), (0, 0), (0, 0)))
    levels = jnp.arange(YBLK, dtype=jnp.int32)

    def add_block(block_id, total):
        first_level = block_id * YBLK
        slab_part = lax.dynamic_slice_in_dim(padded, first_level, YBLK + 2, 2)
        centre = slab_part[:, 1:-1, 1:-1, 1:-1]
        grad_x = 0.5 * (
            slab_part[:, 2:, 1:-1, 1:-1].astype(jnp.float32)
            - slab_part[:, :-2, 1:-1, 1:-1].astype(jnp.float32)
        )
        grad_y = 0.5 * (
            slab_part[:, 1:-1, 2:, 1:-1].astype(jnp.float32)
            - slab_part[:, 1:-1, :-2, 1:-1].astype(jnp.float32)
        )
        grad_z = 0.5 * (
            slab_part[:, 1:-1, 1:-1, 2:].astype(jnp.float32)
            - slab_part[:, 1:-1, 1:-1, :-2].astype(jnp.float32)
        )
        gradient = jnp.stack([grad_x, grad_y, grad_z]).reshape(3, 3, points, size_m)
        flattened = centre.reshape(3, points, size_m)
        picked = jnp.einsum("cqm,mj->cqj", flattened, onehot, preferred_element_type=jnp.float32)
        advected = jnp.einsum("dqj,dcqk->jcqk", picked, gradient, precision=highest).astype(
            jnp.bfloat16
        )
        weight_block = lax.dynamic_slice_in_dim(weight_part, first_level, YBLK, 1)
        live_mask = (first_level + levels)[None, :, None] < live_count
        weighting = jnp.where(live_mask, weight_block, jnp.zeros_like(weight_block)).reshape(points)
        tested = (flattened.astype(jnp.float32) * weighting[None, :, None]).astype(jnp.bfloat16)
        return total + jnp.einsum(
            "cqi,jcqk->jik", tested, advected, preferred_element_type=jnp.float32
        )

    return lax.fori_loop(0, level_cap // YBLK, add_block, running)


def local(modes, weights, counts, mode_index):
    size_m = modes.shape[4]
    window = mode_index.shape[0]
    onehot = (jnp.arange(size_m)[:, None] == mode_index[None, :]).astype(jnp.bfloat16)
    live_count = counts[0]
    extended = padded_2(modes, (("gx", 1), ("gz", 3)), 1)
    running = jnp.zeros((window, size_m, size_m), jnp.float32)
    running = region_terms(extended, weights, live_count, onehot, running)
    partial_sum = lax.psum_scatter(running, "gz", scatter_dimension=1, tiled=True)
    owned = lax.psum(partial_sum, "gx")
    return owned


def solution(mesh):
    placed = (P(None, "gx", None, "gz", None), P("gx", None, "gz"), P(("gx", "gz")), P())
    return jax.shard_map(
        local, mesh=mesh, in_specs=placed, out_specs=P(None, "gz", None), check_vma=False
    )
```

profile of v0, /device:TPU:0, one launch (start us, length us, event | category | flops | bytes accessed | tf_op | source)
XLA Modules:
  0.0 310.6 jit_solution(16225019868388307722)
XLA Ops:
  15.7 4.0 %collective-permute-start.3 = (bf16[3,4,128,1,128]{4,2,3,1,0:T(8,128)(2,1)}, bf16[3,4,128,1,128]{4,2,3,1,0:T(8,128)(2,1)}, u32[]{:S(2)}, u32[]{:S(2)}) collective-permute-start(bf16[3,4,128,1,128]{4,2,3,1,0:T(8,128)(2,1)} %get-tuple-element.190), channel_id=1, source_target_pairs={{1,0},{2,1},{3,2},{4,3},{5,4},{6,5},{7,6},{8,7},{9,8},{10,9},{11,1... | collective-permute-start | bytes 1179656 | tf_op jit(solution)/shard_map/ppermute | solution.py:18
  19.7 13.4 %collective-permute-done.2 = bf16[3,4,128,1,128]{4,2,3,1,0:T(8,128)(2,1)S(1)} collective-permute-done((bf16[3,4,128,1,128]{4,2,3,1,0:T(8,128)(2,1)}, bf16[3,4,128,1,128]{4,2,3,1,0:T(8,128)(2,1)S(1)}, u32[]{:S(2)}, u32[]{:S(2)}) %collective-permute-start.2) | collective-permute-done | bytes 393248 | tf_op jit(solution)/shard_map/ppermute | solution.py:15
  35.0 4.3 %fusion.29 = bf16[3,4,130,10,128]{4,2,3,1,0:T(8,128)(2,1)} fusion(bf16[3,4,128,1,128]{4,2,3,1,0:T(8,128)(2,1)} %collective-permute-done.3, bf16[3,4,128,8,128]{4,2,3,1,0:T(8,128)(2,1)S(1)} %constant_dynamic-update-slice_fusion, bf16[3,4,128,1,128]{4,2,3,1,0:T(8,128)(2,1)S(1)} %collective-permute-done.2), kind=kLoop, calls=%fused_computation.40 | loop fusion | flops 23961600 | bytes 7925760 | tf_op jit(solution)/shard_map/concatenate | solution.py:19
  39.4 165.6 %while.14 = (s32[]{:T(128)}, f32[16,128,128]{1,2,0:T(8,128)}, bf16[3,4,130,10,128]{4,2,3,1,0:T(8,128)(2,1)}, s32[]{:T(128)}, f32[2,128,8]{1,2,0:T(8,128)S(1)}, /...) while((s32[]{:T(128)}, f32[16,128,128]{1,2,0:T(8,128)}, ...), condition=%wide.region_1.2_spmd.clone, body=%wide.region_0.1_spmd.clone.sunk | while | flops 232771744 | bytes 13161326 | solution.py:63
  41.7 3.1 fusion.48
  50.9 3.1 fusion.48
  61.5 3.1 fusion.48
  72.1 3.1 fusion.48
  82.4 3.1 fusion.48
  87.8 2.9 fusion.50
  92.8 3.1 fusion.48
  103.4 3.1 fusion.48
  113.8 3.1 fusion.48
  124.2 3.1 fusion.48
  129.6 2.9 fusion.50
  134.4 3.1 fusion.48
  144.8 3.1 fusion.48
  155.1 3.1 fusion.48
  165.5 3.1 fusion.48
  176.0 3.1 fusion.48
  186.3 3.1 fusion.48
  196.7 3.1 fusion.48
  207.6 78.0 %reduce-scatter.2.cloned.1.call-done = f32[16,8,128]{2,1,0:T(8,128)} async-done(((f32[16,128,128]{2,1,0:T(8,128)}), f32[16,8,128]{2,1,0:T(8,128)}) %reduce-scatter.2.cloned.1.call-update) | async-done | bytes 65552 | tf_op jit(solution)/shard_map/reduce_scatter | solution.py:74
  285.6 16.7 %all-reduce.3.cloned.1.call-done = f32[16,8,128]{2,1,0:T(8,128)} async-done(((f32[16,8,128]{2,1,0:T(8,128)}), f32[16,8,128]{2,1,0:T(8,128)}) %all-reduce.3.cloned.1.call-update) | async-done | bytes 65552 | tf_op jit(solution)/shard_map/psum | solution.py:75
  (232 shorter events, 124.2 us)
Async XLA Ops:
  6.5 279.1 %reduce-scatter.2.cloned.1.call-start = ((), (), s32[]{:S(2)}) async-start(), calls=%async_computation.1 | async-start | bytes 1114112 | tf_op jit(solution)/shard_map/reduce_scatter | solution.py:74
  8.0 2.7 copy-start
  8.2 2.4 collective-permute-start
  8.9 2.9 collective-permute-start.1
  12.8 20.3 %collective-permute-start.2 = (bf16[3,4,128,1,128]{4,2,3,1,0:T(8,128)(2,1)}, bf16[3,4,128,1,128]{4,2,3,1,0:T(8,128)(2,1)S(1)}, u32[]{:S(2)}, u32[]{:S(2)}) collective-permute-start(bf16[3,4,128,1,128]{4,2,3,1,0:T(8,128)(2,1)} %get-tuple-element.189), channel_id=1, source_target_pairs={{0,1},{1,2},{2,3},{3,4},{4,5},{5,6},{6,7},{7,8},{8,9},{9,10},{10,1... | collective-permute-start | bytes 1179656 | tf_op jit(solution)/shard_map/ppermute | solution.py:15
  15.7 19.4 %collective-permute-start.3 = (bf16[3,4,128,1,128]{4,2,3,1,0:T(8,128)(2,1)}, bf16[3,4,128,1,128]{4,2,3,1,0:T(8,128)(2,1)}, u32[]{:S(2)}, u32[]{:S(2)}) collective-permute-start(bf16[3,4,128,1,128]{4,2,3,1,0:T(8,128)(2,1)} %get-tuple-element.190), channel_id=1, source_target_pairs={{1,0},{2,1},{3,2},{4,3},{5,4},{6,5},{7,6},{8,7},{9,8},{10,9},{11,1... | collective-permute-start | bytes 1179656 | tf_op jit(solution)/shard_map/ppermute | solution.py:18
  19.7 19.7 %copy-start.1 = (f32[2,128,8]{1,2,0:T(8,128)S(1)}, f32[2,128,8]{1,2,0:T(8,128)}, u32[]{:S(2)}) copy-start(f32[2,128,8]{1,2,0:T(8,128)} %param.7) | copy-start | bytes 24580
  19.7 19.7 %copy-start.2 = (s32[16]{0:T(128)S(1)}, s32[16]{0:T(128)}, u32[]{:S(2)}) copy-start(s32[16]{0:T(128)} %param.9) | copy-start | bytes 196
  207.5 94.8 %all-reduce.3.cloned.1.call-start = ((), (), s32[]{:S(2)}) async-start(), calls=%async_computation.2 | async-start | bytes 131072 | tf_op jit(solution)/shard_map/psum | solution.py:75
Sparse Core Ops, SparseCore 0:
  207.7 77.9 reduce-scatter.1
  288.0 14.2 all-reduce.2
where the time goes:
time: 313 us; the launch traced here: 311 us
  waiting for transfers between devices  112 us (36%)
  matrix products  96.4 us (31%)
  local copies, waits for them, and re-layouts  61.6 us (20%)
  other arithmetic  18 us (6%)
  between operations  13.5 us (4%)
  starting transfers between devices  7.54 us (2%)
    reduce_scatter x1, waiting for transfers between devices, local(): lax.psum_scatter(running, 'gz', scatter_dimension=1, tiled=True)  78 us
    dot_general x16, matrix products, add_block(): jnp.einsum('dqj,dcqk->jcqk', picked, gradient, precision=highest)  49.4 us
    dot_general x16, matrix products, add_block(): jnp.einsum('cqi,jcqk->jik', tested, advected, preferred_element_type=jnp....  44.6 us
    slice x16, local copies, waits for them, and re-layouts, add_block(): centre = slab_part[:, 1:-1, 1:-1, 1:-1]  29.5 us
    dot_general x16, local copies, waits for them, and re-layouts, add_block(): jnp.einsum('dqj,dcqk->jcqk', picked, gradient, precision=highest)  20.6 us
    psum x1, waiting for transfers between devices, local(): owned = lax.psum(partial_sum, 'gx')  16.7 us
    ppermute x2, waiting for transfers between devices, padded_2(): lax.ppermute(lax.slice_in_dim(block, block.shape[dim] - width, None, axis...  15 us
    lt x16, other arithmetic, add_block(): live_mask = (first_level + levels)[None, :, None] < live_count  10.5 us
  transfers between devices with their start and end apart: 6, of which 6 were waited for; matrix products, arithmetic and copies ran while one was open for 0% of the time, Pallas kernels for 0%

commit v1 on v0

v1 whole, which is shorter than its diff:
```python
import functools

import jax
import jax.numpy as jnp
from jax import lax
from jax.experimental import pallas as pl
from jax.experimental.pallas import tpu as pltpu
from jax.sharding import PartitionSpec as P

LEVELS = 16
UNIT = 16
LANES = 128
VMEM_LIMIT = 48 * 1024 * 1024


def pick_matrix(index_ref, half, comps, size_m):
    lane = lax.broadcasted_iota(jnp.int32, (1, LANES), 1)
    target = jnp.full((1, LANES), -1, jnp.int32)
    for d in range(comps):
        for j in range(half):
            target = jnp.where(lane == d * half + j, index_ref[j] + d * size_m, target)
    row = lax.broadcasted_iota(jnp.int32, (comps * size_m, LANES), 0)
    return jnp.where(row == target, 0.5, 0.0).astype(jnp.bfloat16)


def tested_rows(block, weight_row):
    return (block.astype(jnp.float32).T * weight_row).astype(jnp.bfloat16)


def main_kernel(wrapped, half, span_z, live_ref, index_ref, own_ref, oth_ref, own_w_ref, oth_w_ref, *rest):
    if wrapped:
        acc_ref, pick_ref, picked_ref, adv_ref, test_ref = rest
        edges = ((oth_ref, oth_ref), (own_ref, own_ref))
    else:
        own_edge_ref, oth_edge_ref, acc_ref, pick_ref, picked_ref, adv_ref, test_ref = rest
        edges = ((own_edge_ref, own_edge_ref), (oth_edge_ref, oth_edge_ref))
    comps, span_x, rows, size_m = own_ref.shape
    cap = rows // span_z
    part = LEVELS * span_z
    depth = span_x * part
    per_unit = UNIT // span_z
    pick_ref[...] = pick_matrix(index_ref, half, comps, size_m)
    acc_ref[...] = jnp.zeros_like(acc_ref)
    sub = lax.broadcasted_iota(jnp.int32, (span_z, size_m), 0)

    def plane_refs(which, refs, x):
        body = refs[which]
        other = refs[1 - which]
        if x > 0:
            low = lambda c, r: body[c, x - 1, r]
        elif wrapped:
            low = lambda c, r: other[c, span_x - 1, r]
        else:
            low = lambda c, r: edges[which][0][c, 0, r]
        if x < span_x - 1:
            high = lambda c, r: body[c, x + 1, r]
        elif wrapped:
            high = lambda c, r: other[c, 0, r]
        else:
            high = lambda c, r: edges[which][1][c, 1, r]
        return low, high

    refs = (own_ref, oth_ref)
    weights = (own_w_ref, oth_w_ref)
    for which in range(2):
        body = refs[which]
        live = live_ref[which]

        def block_step(block, carry, which=which, body=body, live=live):
            base = pl.multiple_of(block * part, part)
            spot = pl.ds(base, part)
            wide = []
            for x in range(span_x):
                wide.append(jnp.concatenate([body[d, x, spot] for d in range(comps)], axis=1))
            picked_ref[...] = jnp.dot(
                jnp.concatenate(wide, axis=0), pick_ref[...], preferred_element_type=jnp.float32
            )
            lane = lax.broadcasted_iota(jnp.int32, (1, part), 1)
            mask = (base + lane) < live * span_z
            for x in range(span_x):
                weight_row = jnp.where(mask, weights[which][x, :, spot], 0.0)
                for c in range(comps):
                    test_ref[:, c * depth + x * part : c * depth + (x + 1) * part] = tested_rows(
                        body[c, x, spot], weight_row
                    )
            for x in range(span_x):
                low, high = plane_refs(which, refs, x)

                def unit_step(unit, carry, x=x, low=low, high=high):
                    start = pl.multiple_of(base + unit * UNIT, UNIT)
                    here = pl.ds(start, UNIT)
                    before = pl.ds(pl.multiple_of(jnp.maximum(start - UNIT, 0), UNIT), UNIT)
                    after = pl.ds(pl.multiple_of(jnp.minimum(start + UNIT, rows - UNIT), UNIT), UNIT)
                    has_before = start > 0
                    has_after = start + UNIT < rows
                    grads = []
                    for c in range(comps):
                        mid = body[c, x, here].astype(jnp.float32)
                        down = body[c, x, before].astype(jnp.float32)[UNIT - span_z :]
                        up = body[c, x, after].astype(jnp.float32)[:span_z]
                        down = jnp.where(has_before, down, 0.0)
                        up = jnp.where(has_after, up, 0.0)
                        gx = high(c, here).astype(jnp.float32) - low(c, here).astype(jnp.float32)
                        levels = [down] + [mid[t * span_z : (t + 1) * span_z] for t in range(per_unit)] + [up]
                        for t in range(per_unit):
                            centre = levels[t + 1]
                            gy = levels[t + 2] - levels[t]
                            right = jnp.where(sub == span_z - 1, 0.0, pltpu.roll(centre, span_z - 1, 0))
                            left = jnp.where(sub == 0, 0.0, pltpu.roll(centre, 1, 0))
                            grads.append((gx[t * span_z : (t + 1) * span_z], gy, right - left))
                    local_row = pl.multiple_of(x * part + unit * UNIT, UNIT)
                    picked = picked_ref[pl.ds(local_row, UNIT), :]
                    for j in range(half):
                        outs = [[] for _ in range(comps)]
                        for t in range(per_unit):
                            u = [
                                jnp.broadcast_to(
                                    picked[t * span_z : (t + 1) * span_z, d * half + j : d * half + j + 1],
                                    (span_z, size_m),
                                )
                                for d in range(3)
                            ]
                            for c in range(comps):
                                g = grads[c * per_unit + t]
                                outs[c].append(u[0] * g[0] + u[1] * g[1] + u[2] * g[2])
                        for c in range(comps):
                            value = jnp.concatenate(outs[c], axis=0).astype(jnp.bfloat16)
                            adv_ref[pl.ds(c * depth + local_row, UNIT), j * size_m : (j + 1) * size_m] = value
                    return carry

                lax.fori_loop(0, part // UNIT, unit_step, 0)
            acc_ref[...] += jnp.dot(test_ref[...], adv_ref[...], preferred_element_type=jnp.float32)
            return carry

        lax.fori_loop(0, pl.cdiv(live, LEVELS), block_step, 0)


def seam_kernel(half, index_ref, acc_ref, own_edge_ref, oth_edge_ref, own_last_ref, oth_last_ref, own_w_ref, oth_w_ref, out_ref, adv_ref, total_ref):
    comps, depth, size_m = own_edge_ref.shape
    pieces = out_ref.shape[0]
    owned = size_m // pieces
    pick = pick_matrix(index_ref, half, comps, size_m)[(comps - 1) * size_m :]
    total_ref[...] = acc_ref[...]
    for edge_ref, last_ref, w_ref in (
        (own_edge_ref, own_last_ref, own_w_ref),
        (oth_edge_ref, oth_last_ref, oth_w_ref),
    ):
        for tested_ref, field_ref, w_row, sign in (
            (last_ref, edge_ref, 0, 1.0),
            (edge_ref, last_ref, 1, -1.0),
        ):
            picked = sign * jnp.dot(tested_ref[comps - 1], pick, preferred_element_type=jnp.float32)
            tests = []
            for c in range(comps):
                tests.append(tested_rows(tested_ref[c], w_ref[w_row : w_row + 1, :]))
                field = field_ref[c].astype(jnp.float32)
                for j in range(half):
                    lane = (comps - 1) * half + j
                    adv_ref[c * depth : (c + 1) * depth, j * size_m : (j + 1) * size_m] = (
                        picked[:, lane : lane + 1] * field
                    ).astype(jnp.bfloat16)
            total_ref[...] += jnp.dot(
                jnp.concatenate(tests, axis=1), adv_ref[...], preferred_element_type=jnp.float32
            )
    group = max(1, UNIT // owned)
    for j0 in range(0, half, group):
        parts = [
            total_ref[:, j * size_m : (j + 1) * size_m].reshape(pieces, owned, size_m)
            for j in range(j0, j0 + group)
        ]
        out_ref[:, j0 * owned : (j0 + group) * owned, :] = jnp.concatenate(parts, axis=1).astype(jnp.bfloat16)


def local(modes, weights, counts, mode_index):
    comps, span_x, cap, span_z, size_m = modes.shape
    size_gx, size_gz = lax.axis_size("gx"), lax.axis_size("gz")
    window = mode_index.shape[0]
    half = window // 2
    rows = cap * span_z
    owned = size_m // size_gz
    wrapped = size_gx == 2
    parity = lax.axis_index("gx") % 2
    swap = [(i, i ^ 1) for i in range(size_gx)]
    leftward = [(i, (i - 1) % size_gz) for i in range(size_gz)]

    def other(value):
        return lax.ppermute(value, "gx", swap)

    index_half = lax.dynamic_slice_in_dim(mode_index, parity * half, half)
    own = modes.reshape(comps, span_x, rows, size_m)
    oth = other(own)
    live = jnp.concatenate([counts, other(counts)])
    own_w = weights.reshape(span_x, 1, rows)
    oth_w = other(own_w)
    extra = []
    if not wrapped:
        low = lax.ppermute(own[:, -1:], "gx", [(i, (i + 1) % size_gx) for i in range(size_gx)])
        high = lax.ppermute(own[:, :1], "gx", [(i, (i - 1) % size_gx) for i in range(size_gx)])
        own_edge = jnp.concatenate([low, high], axis=1)
        extra = [own_edge, other(own_edge)]

    masked = jnp.where(jnp.arange(cap)[None, :, None] < counts[0], weights, 0.0)
    depth = span_x * cap
    first = modes[:, :, :, 0].reshape(comps, depth, size_m)
    last = modes[:, :, :, -1].reshape(comps, depth, size_m)
    edge = lax.ppermute(first, "gz", leftward)
    edge_w = lax.ppermute(masked[:, :, 0].reshape(1, depth), "gz", leftward)
    seam_w = jnp.concatenate([masked[:, :, -1].reshape(1, depth), edge_w])

    vmem = pl.BlockSpec(memory_space=pltpu.VMEM)
    smem = pl.BlockSpec(memory_space=pltpu.SMEM)
    block_depth = comps * span_x * LEVELS * span_z
    acc = pl.pallas_call(
        functools.partial(main_kernel, wrapped, half, span_z),
        out_shape=jax.ShapeDtypeStruct((size_m, half * size_m), jnp.float32),
        in_specs=[smem, smem] + [vmem] * (4 + len(extra)),
        out_specs=vmem,
        scratch_shapes=[
            pltpu.VMEM((comps * size_m, LANES), jnp.bfloat16),
            pltpu.VMEM((block_depth // comps, LANES), jnp.float32),
            pltpu.VMEM((block_depth, half * size_m), jnp.bfloat16),
            pltpu.VMEM((size_m, block_depth), jnp.bfloat16),
        ],
        compiler_params=pltpu.CompilerParams(vmem_limit_bytes=VMEM_LIMIT),
    )(live, index_half, own, oth, own_w, oth_w, *extra)

    partial = pl.pallas_call(
        functools.partial(seam_kernel, half),
        out_shape=jax.ShapeDtypeStruct((size_gz, half * owned, size_m), jnp.bfloat16),
        in_specs=[smem] + [vmem] * 7,
        out_specs=vmem,
        scratch_shapes=[
            pltpu.VMEM((comps * depth, half * size_m), jnp.bfloat16),
            pltpu.VMEM((size_m, half * size_m), jnp.float32),
        ],
        compiler_params=pltpu.CompilerParams(vmem_limit_bytes=VMEM_LIMIT),
    )(index_half, acc, edge, other(edge), last, other(last), seam_w, other(seam_w))

    pieces = lax.all_to_all(partial, "gz", 0, 0, tiled=True)
    mine = pieces.astype(jnp.float32).sum(axis=0)
    if wrapped:
        theirs = other(mine)
        both = jnp.where(parity == 0, jnp.stack([mine, theirs]), jnp.stack([theirs, mine]))
    else:
        both = lax.psum(
            jnp.where(jnp.arange(2)[:, None, None] == parity, mine[None], 0.0), "gx"
        )
    return both.reshape(window, owned, size_m)


def solution(mesh):
    placed = (P(None, "gx", None, "gz", None), P("gx", None, "gz"), P(("gx", "gz")), P())
    return jax.shard_map(
        local, mesh=mesh, in_specs=placed, out_specs=P(None, "gz", None), check_vma=False
    )
```

time: 313 us -> 79 us (0.25)
  waiting for transfers between devices: 112 us -> 2.79 us
  matrix products: 96.4 us -> 0 us
  local copies, waits for them, and re-layouts: 61.6 us -> 7.32 us
  Pallas kernels: 0 us -> 28 us
  blocking collectives: 0 us -> 28 us
  other arithmetic: 18 us -> 2 us
  between operations: 13.5 us -> 0.77 us
    dot_general x48 -> x0, matrix products: 96.4 us -> none  [the longest x16 49.4 us: add_block(): jnp.einsum('dqj,dcqk->jcqk', picked, gradient, precision=highest)]
    reduce_scatter x1 -> x0, waiting for transfers between devices: 78 us -> none  [local(): lax.psum_scatter(running, 'gz', scatter_dimension=1, tiled=True)]
    slice x18 -> x1, local copies, waits for them, and re-layouts: 32 us -> 3.31 us  [local(): last = modes[:, :, :, -1].reshape(comps, depth, size_m)]
    pallas_call x0 -> x2, Pallas kernels: none -> 28 us  [the longest x1 24.4 us: local(): pl.pallas_call(functools.partial(main_kernel, wrapped, half, span_z), out...]
    all_to_all x0 -> x1, blocking collectives: none -> 28 us  [local(): pieces = lax.all_to_all(partial, 'gz', 0, 0, tiled=True)]
    dot_general x16 -> x0, local copies, waits for them, and re-layouts: 20.6 us -> none  [add_block(): jnp.einsum('dqj,dcqk->jcqk', picked, gradient, precision=highest)]
    psum x1 -> x0, waiting for transfers between devices: 16.7 us -> none  [local(): owned = lax.psum(partial_sum, 'gx')]
    ppermute x4 -> x9, waiting for transfers between devices: 17.5 us -> 2.79 us  [the longest x1 1.59 us: local(): edge_w = lax.ppermute(masked[:, :, 0].reshape(1, depth), 'gz', leftward)]
  transfers between devices with their start and end apart: 6 -> 9, of which waited for: 6 -> 2; matrix products, arithmetic and copies ran while one was open for 0% -> 11% of each run, Pallas kernels for 0% -> 31%
where the time goes in v1:
time: 79 us; the launch traced here: 77.7 us
  Pallas kernels  28 us (35%)
  blocking collectives  28 us (35%)
  starting transfers between devices  8.81 us (11%)
  local copies, waits for them, and re-layouts  7.32 us (9%)
  waiting for transfers between devices  2.79 us (4%)
  other arithmetic  2 us (3%)
    all_to_all x1, blocking collectives, local(): pieces = lax.all_to_all(partial, 'gz', 0, 0, tiled=True)  28 us
    pallas_call x1, Pallas kernels, local(): pl.pallas_call(functools.partial(main_kernel, wrapped, half, span_z), out...  24.4 us
    ppermute x1, starting transfers between devices, local(): edge = lax.ppermute(first, 'gz', leftward)  6.6 us
    pallas_call x1, Pallas kernels, local(): pl.pallas_call(functools.partial(seam_kernel, half), out_shape=jax.ShapeD...  3.64 us
    slice x1, local copies, waits for them, and re-layouts, local(): last = modes[:, :, :, -1].reshape(comps, depth, size_m)  3.31 us
    unnamed x7, local copies, waits for them, and re-layouts  2.58 us
    ppermute x7, starting transfers between devices, other(): return lax.ppermute(value, 'gx', swap)  1.68 us
    ppermute x1, waiting for transfers between devices, local(): edge_w = lax.ppermute(masked[:, :, 0].reshape(1, depth), 'gz', leftward)  1.59 us
  transfers between devices with their start and end apart: 9, of which 2 were waited for; matrix products, arithmetic and copies ran while one was open for 11% of the time, Pallas kernels for 31%

profile of v1, /device:TPU:0, one launch (start us, length us, event | category | flops | bytes accessed | tf_op | source)
XLA Modules:
  0.0 77.7 jit_solution(11114558159022738575)
XLA Ops:
  0.0 0.5 collective-permute-start.1
  0.5 0.8 %copy.6 = f32[2,128,8]{2,1,0:T(8,128)S(1)} copy(f32[2,128,8]{1,2,0:T(8,128)} %param.5) | data formatting | bytes 16384 | tf_op args[1]
  1.3 0.1 reshape.18.own_w_ref
  1.4 0.2 collective-permute-start.2
  1.6 0.4 collective-permute-start
  2.0 3.3 %fusion = (bf16[3,2,128,1,128]{4,3,2,1,0:T(2,128)(2,1)}, bf16[3,2,128,1,128]{4,3,2,1,0:T(2,128)(2,1)S(1)}) fusion(bf16[3,2,128,8,128]{4,3,2,1,0:T(8,128)(2,1)} %param.4), kind=kLoop, calls=%fused_computation.8 | loop fusion | bytes 786432 | tf_op jit(solution)/shard_map/slice | solution.py:205
  5.3 0.7 copy.11
  6.0 6.6 %collective-permute-start.3 = (bf16[3,256,128]{2,1,0:T(8,128)(2,1)}, bf16[3,256,128]{2,1,0:T(8,128)(2,1)S(1)}, u32[]{:S(2)}, u32[]{:S(2)}) collective-permute-start(bf16[3,256,128]{2,1,0:T(8,128)(2,1)} %bitcast.1), channel_id=1, source_target_pairs={{0,15},{1,0},{2,1},{3,2},{4,3},{5,4},{6,5},{7,6},{8,7},{9,8},{10,9... | collective-permute-start | bytes 589832 | tf_op jit(solution)/shard_map/ppermute | solution.py:206
  13.3 0.6 slice_bitcast_fusion.1
  13.9 0.5 collective-permute-start.6
  14.4 1.0 %copy.12 = bf16[3,2,128,1,128]{4,2,1,0,3:T(8,128)(2,1)S(1)} copy(bf16[3,2,128,1,128]{4,3,2,1,0:T(2,128)(2,1)} %get-tuple-element.5) | data formatting | bytes 393216
  15.5 0.7 dynamic_slice.3.index_ref
  16.2 1.6 %collective-permute-done.6 = f32[1,256]{1,0:T(1,128)} collective-permute-done((f32[1,256]{1,0:T(1,128)}, f32[1,256]{1,0:T(1,128)}, u32[]{:S(2)}, u32[]{:S(2)}) %collective-permute-start.6) | collective-permute-done | bytes 1056 | tf_op jit(solution)/shard_map/ppermute | solution.py:207
  17.8 0.5 collective-permute-start.4
  18.3 0.7 pad_maximum_fusion.own_w_ref
  19.0 0.0 collective-permute-done
  19.0 0.1 collective-permute-start.7
  19.1 0.6 pad_add_fusion.live_ref
  19.7 24.4 %shard_map.46.acc_ref = f32[128,1024]{1,0:T(8,128)S(1)} custom-call(s32[2]{0:T(128)S(1)} %pad_add_fusion.live_ref, s32[8]{0:T(128)S(1)} %dynamic_slice.3.index_ref, bf16[3,2,1024,128]{3,2,1,0:T(8,128)(2,1)S(1)} %bitcast.13, bf16[3,2,1024,128]{3,2,1,0:T(8,128)(2,1)S(1)} %collective-permute-done.1.oth_ref, f32[2,1,1024]{2,1,0:T(1,128)S(1)} %reshape.18.own_w_ref, ...), custom_call_target="tpu_custom_call" | custom-call | tf_op jit(solution)/shard_map/pallas_call | solution.py:213
  44.1 3.6 %shard_map.47 = bf16[16,64,128]{2,1,0:T(8,128)(2,1)S(1)} custom-call(s32[8]{0:T(128)S(1)} %dynamic_slice.3.index_ref, f32[128,1024]{1,0:T(8,128)S(1)} %shard_map.46.acc_ref, bf16[3,256,128]{2,1,0:T(8,128)(2,1)S(1)} %collective-permute-done.3.own_edge_ref, bf16[3,256,128]{2,1,0:T(8,128)(2,1)S(1)} %collective-permute-done.4.oth_edge_ref, ...), custom_call_target="tpu_custom_call" | custom-call | tf_op jit(solution)/shard_map/pallas_call | solution.py:227
  47.8 28.0 %all_to_all.5 = bf16[16,64,128]{2,1,0:T(8,128)(2,1)S(1)} all-to-all(bf16[16,64,128]{2,1,0:T(8,128)(2,1)S(1)} %shard_map.47), channel_id=1, replica_groups=mesh['gx'=2,'gz'=16] {'gz'}, dimensions={0} | all-to-all | bytes 524288 | tf_op jit(solution)/shard_map/all_to_all | solution.py:239
  75.8 0.1 collective-permute-start.8
  75.9 1.2 %collective-permute-done.8 = f32[64,128]{1,0:T(8,128)S(1)} collective-permute-done((f32[64,128]{1,0:T(8,128)S(1)}, f32[64,128]{1,0:T(8,128)S(1)}, u32[]{:S(2)}, u32[]{:S(2)}) %collective-permute-start.8) | collective-permute-done | bytes 32800 | tf_op jit(solution)/shard_map/ppermute | solution.py:187
  77.1 0.6 maximum_select_fusion
  (14 shorter events, 0.1 us)
Async XLA Ops:
  0.0 19.7 %copy-start = (bf16[3,2,128,8,128]{4,3,2,1,0:T(8,128)(2,1)S(1)}, bf16[3,2,128,8,128]{4,3,2,1,0:T(8,128)(2,1)}, u32[]{:S(2)}) copy-start(bf16[3,2,128,8,128]{4,3,2,1,0:T(8,128)(2,1)} %param.4) | copy-start | bytes 4718596
  0.0 13.3 %copy-start.1 = (f32[2,128,8]{1,2,0:T(8,128)S(1)}, f32[2,128,8]{1,2,0:T(8,128)}, u32[]{:S(2)}) copy-start(f32[2,128,8]{1,2,0:T(8,128)} %param.5) | copy-start | bytes 24580
  0.0 19.7 %collective-permute-start.1 = (bf16[3,2,1024,128]{3,2,1,0:T(8,128)(2,1)}, bf16[3,2,1024,128]{3,2,1,0:T(8,128)(2,1)S(1)}, u32[]{:S(2)}, u32[]{:S(2)}) collective-permute-start(bf16[3,2,1024,128]{3,2,1,0:T(8,128)(2,1)} %bitcast.12), channel_id=1, source_target_pairs={{0,16},{16,0},{1,17},{17,1},{2,18},{18,2},{3,19},{19,3},{4,20},{20... | collective-permute-start | bytes 4718600 | tf_op jit(solution)/shard_map/ppermute | solution.py:187
  1.4 18.3 %collective-permute-start.2 = (f32[2,1,1024]{2,1,0:T(1,128)S(1)}, f32[2,1,1024]{2,1,0:T(1,128)S(1)}, u32[]{:S(2)}, u32[]{:S(2)}) collective-permute-start(f32[2,1,1024]{2,1,0:T(1,128)S(1)} %reshape.18.own_w_ref), channel_id=1, source_target_pairs={{0,16},{16,0},{1,17},{17,1},{2,18},{18,2},{3,19},{19,3},{4,20},{20... | collective-permute-start | bytes 24584 | tf_op jit(solution)/shard_map/ppermute | solution.py:187
  1.6 17.4 %collective-permute-start = (s32[1]{0:T(128)}, s32[1]{0:T(128)}, u32[]{:S(2)}, u32[]{:S(2)}) collective-permute-start(s32[1]{0:T(128)} %param.6), channel_id=1, source_target_pairs={{0,16},{16,0},{1,17},{17,1},{2,18},{18,2},{3,19},{19,3},{4,20},{20... | collective-permute-start | bytes 20 | tf_op jit(solution)/shard_map/ppermute | solution.py:187
  6.0 11.8 %collective-permute-start.3 = (bf16[3,256,128]{2,1,0:T(8,128)(2,1)}, bf16[3,256,128]{2,1,0:T(8,128)(2,1)S(1)}, u32[]{:S(2)}, u32[]{:S(2)}) collective-permute-start(bf16[3,256,128]{2,1,0:T(8,128)(2,1)} %bitcast.1), channel_id=1, source_target_pairs={{0,15},{1,0},{2,1},{3,2},{4,3},{5,4},{6,5},{7,6},{8,7},{9,8},{10,9... | collective-permute-start | bytes 589832 | tf_op jit(solution)/shard_map/ppermute | solution.py:206
  13.9 3.9 %collective-permute-start.6 = (f32[1,256]{1,0:T(1,128)}, f32[1,256]{1,0:T(1,128)}, u32[]{:S(2)}, u32[]{:S(2)}) collective-permute-start(f32[1,256]{1,0:T(1,128)} %get-tuple-element.8), channel_id=1, source_target_pairs={{0,15},{1,0},{2,1},{3,2},{4,3},{5,4},{6,5},{7,6},{8,7},{9,8},{10,9... | collective-permute-start | bytes 3080 | tf_op jit(solution)/shard_map/ppermute | solution.py:207
  17.8 26.3 %collective-permute-start.5 = (bf16[3,256,128]{2,1,0:T(8,128)(2,1)S(1)}, bf16[3,256,128]{2,1,0:T(8,128)(2,1)S(1)}, u32[]{:S(2)}, u32[]{:S(2)}) collective-permute-start(bf16[3,256,128]{2,1,0:T(8,128)(2,1)S(1)} %bitcast.14), channel_id=1, source_target_pairs={{0,16},{16,0},{1,17},{17,1},{2,18},{18,2},{3,19},{19,3},{4,20},{20... | collective-permute-start | bytes 589832 | tf_op jit(solution)/shard_map/ppermute | solution.py:187
  17.8 26.3 %collective-permute-start.4 = (bf16[3,256,128]{2,1,0:T(8,128)(2,1)S(1)}, bf16[3,256,128]{2,1,0:T(8,128)(2,1)S(1)}, u32[]{:S(2)}, u32[]{:S(2)}) collective-permute-start(bf16[3,256,128]{2,1,0:T(8,128)(2,1)S(1)} %collective-permute-done.3.own_edge_ref), channel_id=1, source_target_pairs={{0,16},{16,0},{1,17},{17,1},{2,18},{18,2},{3,19},{19,3},{4,20},{20... | collective-permute-start | bytes 589832 | tf_op jit(solution)/shard_map/ppermute | solution.py:187
  19.0 25.1 %collective-permute-start.7 = (f32[2,256]{1,0:T(2,128)S(1)}, f32[2,256]{1,0:T(2,128)S(1)}, u32[]{:S(2)}, u32[]{:S(2)}) collective-permute-start(f32[2,256]{1,0:T(2,128)S(1)} %pad_maximum_fusion.own_w_ref), channel_id=1, source_target_pairs={{0,16},{16,0},{1,17},{17,1},{2,18},{18,2},{3,19},{19,3},{4,20},{20... | collective-permute-start | bytes 6152 | tf_op jit(solution)/shard_map/ppermute | solution.py:187
  75.8 1.3 %collective-permute-start.8 = (f32[64,128]{1,0:T(8,128)S(1)}, f32[64,128]{1,0:T(8,128)S(1)}, u32[]{:S(2)}, u32[]{:S(2)}) collective-permute-start(f32[64,128]{1,0:T(8,128)S(1)} %convert_reduce_fusion), channel_id=1, source_target_pairs={{0,16},{16,0},{1,17},{17,1},{2,18},{18,2},{3,19},{19,3},{4,20},{20... | collective-permute-start | bytes 98312 | tf_op jit(solution)/shard_map/ppermute | solution.py:187
